TPU v7x, 32 devices: a whole 2x2x4 slice. The times are simulated.
32 devices in a mesh: fsdp: 32 (over z, y, x, core).
Axes of the slice: x: 2, y: 2, z: 4, core: 2. Of those that a mesh axis runs over, the one named last changes fastest.
Arguments:
- tokens: bfloat16 [4096, 1024], P('fsdp'), may hold values from -6 to 6
- lengths: int32 [32, 4], P('fsdp'), may hold values from 0 to 128, as said below
- cotangent: bfloat16 [4096, 1024], P('fsdp'), may hold values from -6 to 6
- w_in: bfloat16 [1024, 3352], P('fsdp'), may hold values from -0.1875 to 0.1875
- w_q: bfloat16 [1024, 512], P('fsdp'), may hold values from -0.1875 to 0.1875
- w_k: bfloat16 [1024, 128], P('fsdp'), may hold values from -0.1875 to 0.1875
- w_v: bfloat16 [1024, 128], P('fsdp'), may hold values from -0.1875 to 0.1875
- w_o: bfloat16 [512, 1024], P(None, 'fsdp'), may hold values from -2 to 2
- w_out: bfloat16 [1536, 1024], P(None, 'fsdp'), may hold values from -0.15625 to 0.15625
- w_gate: bfloat16 [1024, 2048], P('fsdp'), may hold values from -0.1875 to 0.1875
- w_up: bfloat16 [1024, 2048], P('fsdp'), may hold values from -0.1875 to 0.1875
- w_down: bfloat16 [2048, 1024], P(None, 'fsdp'), may hold values from -0.125 to 0.125
- gain_a: bfloat16 [1024], P('fsdp'), may hold values from 0.5 to 1.5
- gain_b: bfloat16 [1024], P('fsdp'), may hold values from 0.5 to 1.5
- conv_w: float32 [4, 1792], replicated, may hold values from -3 to 3
- conv_b: float32 [1792], replicated, may hold values from -3 to 3
- dt_bias: float32 [24], replicated, may hold values from -4 to -1
- a_log: float32 [24], replicated, may hold values from -4 to 1
- d_skip: float32 [24], replicated, may hold values from 0.5 to 1.5
Outputs:
- output: bfloat16 [4096, 1024], P('fsdp')
- d_tokens: bfloat16 [4096, 1024], P('fsdp')
- g_w_in: float32 [1024, 3352], P('fsdp')
- g_w_q: float32 [1024, 512], P('fsdp')
- g_w_k: float32 [1024, 128], P('fsdp')
- g_w_v: float32 [1024, 128], P('fsdp')
- g_w_o: float32 [512, 1024], P(None, 'fsdp')
- g_w_out: float32 [1536, 1024], P(None, 'fsdp')
- g_w_gate: float32 [1024, 2048], P('fsdp')
- g_w_up: float32 [1024, 2048], P('fsdp')
- g_w_down: float32 [2048, 1024], P(None, 'fsdp')
- g_gain_a: float32 [1024], P('fsdp')
- g_gain_b: float32 [1024], P('fsdp')
- g_conv_w: float32 [4, 1792], replicated
- g_conv_b: float32 [1792], replicated
- g_dt_bias: float32 [24], replicated
- g_a_log: float32 [24], replicated
- g_d_skip: float32 [24], replicated
Inputs may be any that keep to these rules, and one draw needn't show every extreme that they name: Row p lists the lengths of the sequences on device p in order: nonzero entries come first, each 32 or more, and they sum to 128; zeros mark unused slots.
All inputs are finite; a program needn't handle non-finite values.
Results may differ from a plain program's by a relative error of at most 0.012.
Values may be sent and summed in bfloat16 or wider, within the bound.
A program may use at most 256 MiB of HBM per device.

v0:
```python
import jax
import jax.numpy as jnp
from jax import lax
from jax.sharding import PartitionSpec as P

FF = 2048
STATE = 128
Q_HEADS = 8
KV_HEADS = 2
HEAD_DIM = 64
DSSM = 1536
CONV = 1792
DIN = 3352
QD = 512
KD = 128


norm_eps = 1e-05
rope_base = 100000000000.0


def segment_layout(lengths_row, row_count):
    seq_ends = jnp.cumsum(lengths_row)
    seq_starts = seq_ends - lengths_row
    places = jnp.arange(row_count, dtype=jnp.int32)
    segment = jnp.sum((places[:, None] >= seq_ends[None, :]).astype(jnp.int32), axis=1)
    picked = (
        segment[:, None] == jnp.arange(lengths_row.shape[0], dtype=jnp.int32)[None, :]
    ).astype(jnp.int32)
    position = places - jnp.sum(picked * seq_starts[None, :], axis=1)
    return (segment, position)


def rms_scaled(values, gain_row):
    return (
        values
        * lax.rsqrt(jnp.mean(values * values, axis=1, keepdims=True) + norm_eps)
        * gain_row[None, :]
    )


def rotate(values, position):
    half_dim = values.shape[-1] // 2
    ladder = jnp.arange(half_dim, dtype=jnp.float32) * (-2.0 / values.shape[-1])
    inverse = jnp.power(jnp.float32(rope_base), ladder)
    angles = position.astype(jnp.float32)[:, None] * inverse[None, :]
    cosine = jnp.cos(angles)[:, None, :]
    sine_rows = jnp.sin(angles)[:, None, :]
    half_one = values[..., :half_dim]
    second = values[..., half_dim:]
    return jnp.concatenate(
        [half_one * cosine - second * sine_rows, second * cosine + half_one * sine_rows], axis=-1
    )


def causal_conv(xbc_in, segment, conv_weight, conv_bias):
    row_count = xbc_in.shape[0]
    taps = conv_weight.shape[0]
    conv_sum = jnp.zeros_like(xbc_in) + conv_bias[None, :]
    for tap_index in range(taps):
        lag_rows = taps - 1 - tap_index
        shifted = jnp.pad(xbc_in, ((lag_rows, 0), (0, 0)))[:row_count]
        seg_shift = jnp.pad(segment, (lag_rows, 0), constant_values=-1)[:row_count]
        keep_rows = (seg_shift == segment).astype(xbc_in.dtype)
        conv_sum = conv_sum + conv_weight[tap_index][None, :] * shifted * keep_rows[:, None]
    return conv_sum


def mamba_inputs(xbc_in, dt_in, segment, conv_weight, conv_bias, dt_shift, a_logs):
    activated = jax.nn.silu(causal_conv(xbc_in, segment, conv_weight, conv_bias))
    row_count = xbc_in.shape[0]
    head_count = dt_shift.shape[0]
    x_heads = activated[:, :DSSM].reshape(row_count, head_count, DSSM // head_count)
    b_state = activated[:, DSSM : DSSM + STATE]
    c_state = activated[:, DSSM + STATE :]
    dt_step = jax.nn.softplus(dt_in + dt_shift[None, :])
    log_decay = -jnp.exp(a_logs)[None, :] * dt_step
    running = jnp.cumsum(log_decay, axis=0).T
    places = jnp.arange(row_count)
    causal = (segment[:, None] == segment[None, :]) & (places[:, None] >= places[None, :])
    gap_log = running[:, :, None] - running[:, None, :]
    decay_mask = jnp.exp(jnp.where(causal[None], gap_log, -10000.0))
    return (x_heads, b_state, c_state, dt_step, decay_mask)


def gated_out(y_heads, x_heads, z_gate, skip_rates):
    row_count = y_heads.shape[0]
    y_flat = (y_heads + skip_rates[None, :, None] * x_heads).reshape(row_count, -1)
    return y_flat * jax.nn.silu(z_gate)


def swiglu(gate_pre, upward):
    return jax.nn.silu(gate_pre) * upward


def forward_prod(rows_in, weight):
    return jnp.dot(rows_in, weight, preferred_element_type=jnp.float32)


def outer_sum(left_rows, right_rows):
    return lax.dot_general(
        left_rows, right_rows, (((0,), (0,)), ((), ())), preferred_element_type=jnp.float32
    )


def back_prod(grad_rows, weight):
    return lax.dot_general(
        grad_rows, weight, (((1,), (1,)), ((), ())), preferred_element_type=jnp.float32
    )


def grad_block(left_full, right_rows, gain_grad, right_back, back_full):
    return jnp.concatenate(
        [outer_sum(left_full, right_rows), gain_grad[:, None], outer_sum(back_full, right_back)],
        axis=1,
    )


def per_device(
    tokens,
    lengths,
    cotangent,
    w_in,
    w_q,
    w_k,
    w_v,
    w_o,
    w_out,
    w_gate,
    w_up,
    w_down,
    gain_a,
    gain_b,
    conv_w,
    conv_b,
    dt_bias,
    a_log,
    d_skip,
):
    gathered = (
        lax.all_gather(w_in, "fsdp", axis=0, tiled=True),
        lax.all_gather(w_q, "fsdp", axis=0, tiled=True),
        lax.all_gather(w_k, "fsdp", axis=0, tiled=True),
        lax.all_gather(w_v, "fsdp", axis=0, tiled=True),
        lax.all_gather(w_gate, "fsdp", axis=0, tiled=True),
        lax.all_gather(w_up, "fsdp", axis=0, tiled=True),
        lax.all_gather(gain_a, "fsdp", axis=0, tiled=True),
        lax.all_gather(gain_b, "fsdp", axis=0, tiled=True),
        lax.all_gather(w_o, "fsdp", axis=1, tiled=True),
        lax.all_gather(w_out, "fsdp", axis=1, tiled=True),
        lax.all_gather(w_down, "fsdp", axis=1, tiled=True),
    )
    (
        full_in,
        full_q,
        full_k,
        full_v,
        full_gate,
        full_up,
        full_ga,
        full_gb,
        full_o,
        full_out,
        full_down,
    ) = gathered
    row_count = tokens.shape[0]
    segment, position = segment_layout(lengths[0], row_count)
    places = jnp.arange(row_count)
    causal = (segment[:, None] == segment[None, :]) & (places[:, None] >= places[None, :])
    resid_in = tokens.astype(jnp.float32)
    normed_f, norm_back_a = jax.vjp(rms_scaled, resid_in, full_ga.astype(jnp.float32))
    normed = normed_f.astype(jnp.bfloat16)
    zxd = forward_prod(normed, full_in)
    q_raw = forward_prod(normed, full_q)
    k_raw = forward_prod(normed, full_k)
    v_low = forward_prod(normed, full_v).astype(jnp.bfloat16)
    z_gate = zxd[:, :DSSM]
    xbc_in = zxd[:, DSSM : DSSM + CONV]
    dt_raw = zxd[:, DSSM + CONV :]

    def pre_part(xbc_part, dt_part, conv_weight, conv_bias, dt_shift, a_logs):
        return mamba_inputs(xbc_part, dt_part, segment, conv_weight, conv_bias, dt_shift, a_logs)

    (x_heads, b_state, c_state, dt_step, decay_mask), pre_back = jax.vjp(
        pre_part, xbc_in, dt_raw, conv_w, conv_b, dt_bias, a_log
    )
    b_low = b_state.astype(jnp.bfloat16)
    c_low = c_state.astype(jnp.bfloat16)
    gram_cb = lax.dot_general(
        c_low, b_low, (((1,), (1,)), ((), ())), preferred_element_type=jnp.float32
    )
    mix_low = (gram_cb[None] * decay_mask).astype(jnp.bfloat16)
    vals_low = (dt_step[:, :, None] * x_heads).astype(jnp.bfloat16)
    y_heads = jnp.einsum("hts,shp->thp", mix_low, vals_low, preferred_element_type=jnp.float32)
    gated_f, post_back = jax.vjp(gated_out, y_heads, x_heads, z_gate, d_skip)
    gated_low = gated_f.astype(jnp.bfloat16)

    def rope_pair(q_part, k_part):
        return (
            rotate(q_part.reshape(row_count, Q_HEADS, HEAD_DIM), position),
            rotate(k_part.reshape(row_count, KV_HEADS, HEAD_DIM), position),
        )

    (q_rot, k_rot), rope_back = jax.vjp(rope_pair, q_raw, k_raw)
    group_size = Q_HEADS // KV_HEADS
    q_low = q_rot.astype(jnp.bfloat16).reshape(row_count, KV_HEADS, group_size, HEAD_DIM)
    k_low = k_rot.astype(jnp.bfloat16)
    v_group = v_low.reshape(row_count, KV_HEADS, HEAD_DIM)
    score_scale = HEAD_DIM ** (-0.5)

    def masked_scores():
        raw_scores = (
            jnp.einsum("tkgd,skd->kgts", q_low, k_low, preferred_element_type=jnp.float32)
            * score_scale
        )
        return jnp.where(causal[None, None], raw_scores, -1000000000.0)

    masked = masked_scores()
    row_peak = jnp.max(masked, axis=-1, keepdims=True)
    row_total = jnp.sum(jnp.exp(masked - row_peak), axis=-1, keepdims=True)
    prob_rows = jnp.exp(masked - row_peak) / row_total
    attended = jnp.einsum(
        "kgts,skd->tkgd",
        prob_rows.astype(jnp.bfloat16),
        v_group,
        preferred_element_type=jnp.float32,
    )
    context = attended.astype(jnp.bfloat16).reshape(row_count, QD)
    attn_out = forward_prod(context, full_o)
    mamba_out = forward_prod(gated_low, full_out)
    mid_sum = resid_in + attn_out + mamba_out
    normed_bf, norm_back_b = jax.vjp(rms_scaled, mid_sum, full_gb.astype(jnp.float32))
    normed_b = normed_bf.astype(jnp.bfloat16)
    gate_pre = forward_prod(normed_b, full_gate)
    upward = forward_prod(normed_b, full_up)
    hidden_f, glu_back = jax.vjp(swiglu, gate_pre, upward)
    hidden = hidden_f.astype(jnp.bfloat16)
    result = (mid_sum + forward_prod(hidden, full_down)).astype(jnp.bfloat16)
    regathered = (
        lax.all_gather(w_in, "fsdp", axis=0, tiled=True),
        lax.all_gather(w_q, "fsdp", axis=0, tiled=True),
        lax.all_gather(w_k, "fsdp", axis=0, tiled=True),
        lax.all_gather(w_v, "fsdp", axis=0, tiled=True),
        lax.all_gather(w_gate, "fsdp", axis=0, tiled=True),
        lax.all_gather(w_up, "fsdp", axis=0, tiled=True),
        lax.all_gather(w_o, "fsdp", axis=1, tiled=True),
        lax.all_gather(w_out, "fsdp", axis=1, tiled=True),
        lax.all_gather(w_down, "fsdp", axis=1, tiled=True),
    )
    back_in, back_q, back_k, back_v, back_gate, back_up, back_o, back_out, back_down = regathered
    grad_top = cotangent.astype(jnp.float32)
    d_hidden = back_prod(cotangent, back_down)
    d_gate_f, d_up_f = glu_back(d_hidden)
    d_gate = d_gate_f.astype(jnp.bfloat16)
    d_up = d_up_f.astype(jnp.bfloat16)
    d_glu = jnp.concatenate([d_gate, d_up], axis=1)
    d_normed_b = back_prod(d_gate, back_gate) + back_prod(d_up, back_up)
    d_mid_norm, g_gain_b = norm_back_b(d_normed_b)
    d_mid = grad_top + d_mid_norm
    d_branch = d_mid.astype(jnp.bfloat16)
    d_context = back_prod(d_branch, back_o)
    d_gated = back_prod(d_branch, back_out)
    d_att_low = d_context.reshape(row_count, KV_HEADS, group_size, HEAD_DIM).astype(jnp.bfloat16)
    masked_again = masked_scores()
    prob_again = jnp.exp(masked_again - row_peak) / row_total
    prob_low = prob_again.astype(jnp.bfloat16)
    d_values = jnp.einsum("kgts,tkgd->skd", prob_low, d_att_low, preferred_element_type=jnp.float32)
    d_probs = jnp.einsum("tkgd,skd->kgts", d_att_low, v_group, preferred_element_type=jnp.float32)
    d_scores = (
        prob_again * (d_probs - jnp.sum(d_probs * prob_again, axis=-1, keepdims=True))
    ).astype(jnp.bfloat16)
    d_q_rot = (
        jnp.einsum("kgts,skd->tkgd", d_scores, k_low, preferred_element_type=jnp.float32)
        * score_scale
    )
    d_k_rot = (
        jnp.einsum("kgts,tkgd->skd", d_scores, q_low, preferred_element_type=jnp.float32)
        * score_scale
    )
    d_q_raw, d_k_raw = rope_back((d_q_rot.reshape(row_count, Q_HEADS, HEAD_DIM), d_k_rot))
    d_q_low = d_q_raw.astype(jnp.bfloat16)
    d_k_low = d_k_raw.astype(jnp.bfloat16)
    d_v_low = d_values.reshape(row_count, KD).astype(jnp.bfloat16)
    d_y_heads, d_x_post, d_z, g_skip = post_back(d_gated)
    d_y_low = d_y_heads.astype(jnp.bfloat16)
    d_mix = jnp.einsum("thp,shp->hts", d_y_low, vals_low, preferred_element_type=jnp.float32)
    d_vals = jnp.einsum("hts,thp->shp", mix_low, d_y_low, preferred_element_type=jnp.float32)
    d_gram = jnp.sum(d_mix * decay_mask, axis=0).astype(jnp.bfloat16)
    d_decay = d_mix * gram_cb[None]
    d_step = jnp.sum(d_vals * x_heads, axis=2)
    d_x_heads = d_x_post + d_vals * dt_step[:, :, None]
    d_c_state = jnp.dot(d_gram, b_low, preferred_element_type=jnp.float32)
    d_b_state = outer_sum(d_gram, c_low)
    d_xbc, d_dt_raw, g_conv_w, g_conv_b, g_dt_bias, g_a_log = pre_back(
        (d_x_heads, d_b_state, d_c_state, d_step, d_decay)
    )
    d_zxd = jnp.concatenate([d_z, d_xbc, d_dt_raw], axis=1).astype(jnp.bfloat16)
    d_proj = jnp.concatenate([d_zxd, d_q_low, d_k_low, d_v_low], axis=1)
    d_normed = (
        back_prod(d_zxd, back_in)
        + back_prod(d_q_low, back_q)
        + back_prod(d_k_low, back_k)
        + back_prod(d_v_low, back_v)
    )
    d_resid, g_gain_a = norm_back_a(d_normed)
    d_tokens = (d_mid + d_resid).astype(jnp.bfloat16)
    mixed_outs = jnp.concatenate([context, gated_low], axis=1)
    sum_conv_w, sum_conv_b, sum_dt_bias, sum_a_log, sum_skip = lax.psum(
        (g_conv_w, g_conv_b, g_dt_bias, g_a_log, g_skip), "fsdp"
    )
    all_rows = lax.psum_scatter(
        jnp.concatenate(
            [
                grad_block(normed_b, d_glu, g_gain_b, hidden, cotangent),
                grad_block(normed, d_proj, g_gain_a, mixed_outs, d_branch),
            ],
            axis=1,
        ),
        "fsdp",
        scatter_dimension=0,
        tiled=True,
    )
    ffn_cols = 3 * FF + 1
    ffn_rows = all_rows[:, :ffn_cols]
    mixer_rows = all_rows[:, ffn_cols:]
    sum_gate = ffn_rows[:, :FF]
    sum_up = ffn_rows[:, FF : 2 * FF]
    sum_gain_b = ffn_rows[:, 2 * FF]
    sum_down = ffn_rows[:, 2 * FF + 1 :].T
    proj_cols = DIN + QD + 2 * KD
    sum_in = mixer_rows[:, :DIN]
    sum_q = mixer_rows[:, DIN : DIN + QD]
    sum_k = mixer_rows[:, DIN + QD : DIN + QD + KD]
    sum_v = mixer_rows[:, DIN + QD + KD : proj_cols]
    sum_gain_a = mixer_rows[:, proj_cols]
    sum_o = mixer_rows[:, proj_cols + 1 : proj_cols + 1 + QD].T
    sum_out = mixer_rows[:, proj_cols + 1 + QD :].T
    return (
        result,
        d_tokens,
        sum_in,
        sum_q,
        sum_k,
        sum_v,
        sum_o,
        sum_out,
        sum_gate,
        sum_up,
        sum_down,
        sum_gain_a,
        sum_gain_b,
        sum_conv_w,
        sum_conv_b,
        sum_dt_bias,
        sum_a_log,
        sum_skip,
    )


def solution(mesh):
    in_specs = (
        P("fsdp", None),
        P("fsdp", None),
        P("fsdp", None),
        P("fsdp", None),
        P("fsdp", None),
        P("fsdp", None),
        P("fsdp", None),
        P(None, "fsdp"),
        P(None, "fsdp"),
        P("fsdp", None),
        P("fsdp", None),
        P(None, "fsdp"),
        P("fsdp"),
        P("fsdp"),
        P(),
        P(),
        P(),
        P(),
        P(),
    )
    out_specs = (
        P("fsdp", None),
        P("fsdp", None),
        P("fsdp", None),
        P("fsdp", None),
        P("fsdp", None),
        P("fsdp", None),
        P(None, "fsdp"),
        P(None, "fsdp"),
        P("fsdp", None),
        P("fsdp", None),
        P(None, "fsdp"),
        P("fsdp"),
        P("fsdp"),
        P(),
        P(),
        P(),
        P(),
        P(),
    )
    return jax.shard_map(
        per_device, mesh=mesh, in_specs=in_specs, out_specs=out_specs, check_vma=False
    )
```

profile of v0, /device:TPU:1, one launch (start us, length us, event | category | flops | bytes accessed | tf_op | source)
XLA Modules:
  0.0 1257.9 jit_solution(8249927849902323648)
XLA Ops:
  13.7 40.6 %all-reduce.23 = (bf16[1024]{0:T(1024)(128)(2,1)S(1)}, bf16[1024]{0:T(1024)(128)(2,1)S(1)}) all-reduce(bf16[1024]{0:T(1024)(128)(2,1)S(1)} %dynamic-update-slice, bf16[1024]{0:T(1024)(128)(2,1)S(1)} %dynamic-update-slice.1), channel_id=1, replica_groups=mesh['fsdp'=32] {'fsdp'}, use_global_device_ids=true, to_apply=%add.20 | all-reduce | flops 2048 | bytes 8192
  58.4 42.7 %all_gather.44 = bf16[1024,128]{1,0:T(8,128)(2,1)S(1)} all-gather(bf16[32,128]{1,0:T(8,128)(2,1)} %param.24), channel_id=1, replica_groups=mesh['fsdp'=32] {'fsdp'}, dimensions={0}, use_global_device_ids=true | all-gather | bytes 270336 | tf_op jit(solution)/shard_map/all_gather | solution.py:143
  101.0 37.7 %all_gather.43 = bf16[1024,128]{1,0:T(8,128)(2,1)S(1)} all-gather(bf16[32,128]{1,0:T(8,128)(2,1)} %param.25), channel_id=1, replica_groups=mesh['fsdp'=32] {'fsdp'}, dimensions={0}, use_global_device_ids=true | all-gather | bytes 270336 | tf_op jit(solution)/shard_map/all_gather | solution.py:144
  147.2 50.0 %all-gather.12.cloned.1.call-done = bf16[1024,3352]{1,0:T(8,128)(2,1)} async-done(((bf16[32,3352]{1,0:T(8,128)(2,1)}), bf16[1024,3352]{1,0:T(8,128)(2,1)}) %all-gather.12.cloned.1.call-update) | async-done | bytes 6864912 | tf_op jit(solution)/shard_map/all_gather | solution.py:141
  197.2 5.9 fusion.106
  205.1 3.3 fusion.118
  212.1 45.3 %all-gather.14.cloned.1.call-done = bf16[1536,1024]{0,1:T(8,128)(2,1)} async-done(((bf16[1536,32]{0,1:T(8,128)(2,1)}), bf16[1536,1024]{0,1:T(8,128)(2,1)}) %all-gather.14.cloned.1.call-update) | async-done | bytes 3145744 | tf_op jit(solution)/shard_map/all_gather | solution.py:150
  257.5 3.1 multiply_reduce_fusion.10
  260.8 60.3 %all-gather.18.cloned.1.call-done = bf16[1024,2048]{1,0:T(8,128)(2,1)} async-done(((bf16[32,2048]{1,0:T(8,128)(2,1)}), bf16[1024,2048]{1,0:T(8,128)(2,1)}) %all-gather.18.cloned.1.call-update) | async-done | bytes 4194320 | tf_op jit(solution)/shard_map/all_gather | solution.py:146
  321.1 3.9 fusion.124
  325.0 59.4 %all-gather.16.cloned.1.call-done = bf16[1024,2048]{1,0:T(8,128)(2,1)} async-done(((bf16[32,2048]{1,0:T(8,128)(2,1)}), bf16[1024,2048]{1,0:T(8,128)(2,1)}) %all-gather.16.cloned.1.call-update) | async-done | bytes 4194320 | tf_op jit(solution)/shard_map/all_gather | solution.py:145
  384.4 3.9 fusion.123
  388.3 59.6 %all-gather.20.cloned.1.call-done = bf16[2048,1024]{0,1:T(8,128)(2,1)} async-done(((bf16[2048,32]{0,1:T(8,128)(2,1)}), bf16[2048,1024]{0,1:T(8,128)(2,1)}) %all-gather.20.cloned.1.call-update) | async-done | bytes 4194320 | tf_op jit(solution)/shard_map/all_gather | solution.py:151
  447.9 5.0 multiply_convert_fusion.1
  459.0 2.9 multiply_reduce_fusion.5
  477.7 4.5 fusion.60
  482.2 8.1 fusion.15
  507.6 4.6 convolution_bitcast_fusion
  512.2 8.3 fusion.104
  524.1 124.0 %concatenate.38 = f32[1024,12314]{0,1:T(8,128)} concatenate(f32[1024,4096]{0,1:T(8,128)} %fusion.15, f32[1024,1]{0,1:T(1,128)S(1)} %bitcast.187, f32[1024,2048]{0,1:T(8,128)} %convolution_bitcast_fusion, f32[1024,4120]{0,1:T(8,128)} %fusion.104, f32[1024,1]{0,1:T(1,128)S(1)} %bitcast.188, f32[1024,2048]{0,1:T(8,128)} %fusion.60), dimensions={1} | concatenate | bytes 100876288 | tf_op jit(solution)/shard_map/concatenate | solution.py:312
  648.1 49.8 %copy.168 = f32[1024,12314]{1,0:T(8,128)} copy(f32[1024,12314]{0,1:T(8,128)} %concatenate.38) | data formatting | bytes 100876288
  699.0 67.8 %all-reduce.22 = (f32[4,1792]{1,0:T(4,128)}, f32[1792]{0:T(1024)}, f32[24]{0:T(128)}, f32[24]{0:T(128)}, f32[24]{0:T(128)}) all-reduce(f32[4,1792]{1,0:T(4,128)S(1)} %pad_add_fusion, f32[1792]{0:T(1024)S(1)} %copy-done.63, f32[24]{0:T(128)S(1)} %copy-done.94, f32[24]{0:T(128)S(1)} %negate_multiply_fusion, ...), channel_id=1, replica_groups=mesh['fsdp'=32] {'fsdp'}, use_global_device_ids=true, to_apply=%region_23.24 | all-reduce | flops 9032 | bytes 72256 | tf_op jit(solution)/shard_map/psum | solution.py:308
  767.7 4.6 fusion.8
  772.2 467.5 %reduce-scatter.4.cloned.1.call-done = f32[32,12314]{1,0:T(8,128)} async-done(((f32[1024,12314]{1,0:T(8,128)}), f32[32,12314]{1,0:T(8,128)}) %reduce-scatter.4.cloned.1.call-update) | async-done | bytes 1576208
  (328 shorter events, 79.3 us)
Async XLA Ops:
  7.2 133.0 %copy-start.2 = (bf16[128,1024]{1,0:T(8,128)(2,1)S(1)}, bf16[128,1024]{1,0:T(8,128)(2,1)}, u32[]{:S(2)}) copy-start(bf16[128,1024]{1,0:T(8,128)(2,1)} %param.19) | copy-start | bytes 786436
  7.2 132.7 %copy-start.103 = (f32[24]{0:T(128)S(1)}, f32[24]{0:T(128)}, u32[]{:S(2)}) copy-start(f32[24]{0:T(128)} %param.36) | copy-start | bytes 292
  7.2 133.8 %all-gather.8.cloned.1.call-start = ((), (), s32[]{:S(2)}) async-start(), calls=%async_computation.1 | async-start | bytes 1081344 | tf_op jit(solution)/shard_map/all_gather | solution.py:142
  7.9 136.7 %all-gather.10.cloned.1.call-start = ((), (), s32[]{:S(2)}) async-start(), calls=%async_computation.2 | async-start | bytes 1081344 | tf_op jit(solution)/shard_map/all_gather | solution.py:149
  8.7 188.5 %all-gather.12.cloned.1.call-start = ((), (), s32[]{:S(2)}) async-start(), calls=%async_computation.3 | async-start | bytes 7299072 | tf_op jit(solution)/shard_map/all_gather | solution.py:141
  9.4 248.1 %all-gather.14.cloned.1.call-start = ((), (), s32[]{:S(2)}) async-start(), calls=%async_computation.4 | async-start | bytes 3244032 | tf_op jit(solution)/shard_map/all_gather | solution.py:150
  10.0 311.1 %all-gather.18.cloned.1.call-start = ((), (), s32[]{:S(2)}) async-start(), calls=%async_computation.6 | async-start | bytes 4325376 | tf_op jit(solution)/shard_map/all_gather | solution.py:146
  10.6 373.8 %all-gather.16.cloned.1.call-start = ((), (), s32[]{:S(2)}) async-start(), calls=%async_computation.5 | async-start | bytes 4325376 | tf_op jit(solution)/shard_map/all_gather | solution.py:145
  11.2 436.7 %all-gather.20.cloned.1.call-start = ((), (), s32[]{:S(2)}) async-start(), calls=%async_computation.7 | async-start | bytes 4325376 | tf_op jit(solution)/shard_map/all_gather | solution.py:151
  11.9 1227.8 %reduce-scatter.4.cloned.1.call-start = ((), (), s32[]{:S(2)}) async-start(), calls=%async_computation.8 | async-start | bytes 52445184
  55.9 88.2 %copy-start.52 = (pred[128,128]{0,1:T(8,128)(4,1)}, pred[128,128]{0,1:T(8,128)(4,1)S(1)}, u32[]{:S(2)}) copy-start(pred[128,128]{0,1:T(8,128)(4,1)S(1)} %fusion.71) | copy-start | bytes 49156
  58.3 146.6 %copy-start.42 = (f32[1792]{0:T(1024)}, f32[1792]{0:T(1024)S(1)}, u32[]{:S(2)}) copy-start(f32[1792]{0:T(1024)S(1)} %get-tuple-element.104) | copy-start | bytes 21508
  58.3 146.6 %copy-start.44 = (f32[1792]{0:T(1024)}, f32[1792]{0:T(1024)S(1)}, u32[]{:S(2)}) copy-start(f32[1792]{0:T(1024)S(1)} %get-tuple-element.102) | copy-start | bytes 21508
  58.3 146.6 %copy-start.46 = (f32[1792]{0:T(1024)}, f32[1792]{0:T(1024)S(1)}, u32[]{:S(2)}) copy-start(f32[1792]{0:T(1024)S(1)} %get-tuple-element.103) | copy-start | bytes 21508
  58.3 146.6 %copy-start.48 = (f32[1792]{0:T(1024)}, f32[1792]{0:T(1024)S(1)}, u32[]{:S(2)}) copy-start(f32[1792]{0:T(1024)S(1)} %get-tuple-element.105) | copy-start | bytes 21508
  139.9 63.3 %copy-start.92 = (f32[24]{0:T(128)}, f32[24]{0:T(128)S(1)}, u32[]{:S(2)}) copy-start(f32[24]{0:T(128)S(1)} %exponential_negate_fusion) | copy-start | bytes 292
  140.1 64.9 %copy-start.80 = (f32[128]{0:T(128)}, f32[128]{0:T(128)S(1)}, u32[]{:S(2)}) copy-start(f32[128]{0:T(128)S(1)} %get-tuple-element.156) | copy-start | bytes 1540
  140.1 64.9 %copy-start.82 = (f32[128]{0:T(128)}, f32[128]{0:T(128)S(1)}, u32[]{:S(2)}) copy-start(f32[128]{0:T(128)S(1)} %get-tuple-element.157) | copy-start | bytes 1540
  140.1 65.0 %copy-start.84 = (f32[128]{0:T(128)}, f32[128]{0:T(128)S(1)}, u32[]{:S(2)}) copy-start(f32[128]{0:T(128)S(1)} %get-tuple-element.158) | copy-start | bytes 1540
  260.6 60.4 %copy-start.99 = (f32[128]{0:T(128)}, f32[128]{0:T(128)S(1)}, u32[]{:S(2)}) copy-start(f32[128]{0:T(128)S(1)} %get-tuple-element.161) | copy-start | bytes 1540
  260.7 60.4 %copy-start.86 = (f32[128]{0:T(128)}, f32[128]{0:T(128)S(1)}, u32[]{:S(2)}) copy-start(f32[128]{0:T(128)S(1)} %fusion.87) | copy-start | bytes 1540
  325.0 122.9 %copy-start.19 = (bf16[128,1024]{1,0:T(8,128)(2,1)S(1)}, bf16[128,1024]{1,0:T(8,128)(2,1)}, u32[]{:S(2)}) copy-start(bf16[128,1024]{1,0:T(8,128)(2,1)} %param.21) | copy-start | bytes 786436
  698.0 68.8 %copy-start.96 = (f32[128]{0:T(128)S(1)}, f32[128]{0:T(128)}, u32[]{:S(2)}) copy-start(f32[128]{0:T(128)} %copy-done.95) | copy-start | bytes 1540
  698.0 68.8 %copy-start.98 = (f32[128]{0:T(128)S(1)}, f32[128]{0:T(128)}, u32[]{:S(2)}) copy-start(f32[128]{0:T(128)} %get-tuple-element.101) | copy-start | bytes 1540
  (92 other events, 565.1 us)
Sparse Core Ops, SparseCore 0:
  10.9 56.1 all-gather.7
  70.0 53.0 all-gather.9
  126.0 71.2 all-gather.11
  200.0 57.4 all-gather.13
  260.2 60.8 all-gather.17
  323.8 60.5 all-gather.15
  387.3 60.5 all-gather.19
  698.1 541.5 reduce-scatter.3
where the time goes:
time: 1270 us; the launch traced here: 1260 us
  waiting for transfers between devices  746 us (59%)
  local copies, waits for them, and re-layouts  200 us (16%)
  blocking collectives  189 us (15%)
  matrix products  85.1 us (7%)
  other arithmetic  20.9 us (2%)
  between operations  16 us (1%)
    unnamed x9, waiting for transfers between devices  472 us
    concatenate x1, local copies, waits for them, and re-layouts, per_device(): jnp.concatenate([grad_block(normed_b, d_glu, g_gain_b, hidden, cotangent)...  124 us
    psum x1, blocking collectives, per_device(): lax.psum((g_conv_w, g_conv_b, g_dt_bias, g_a_log, g_skip), 'fsdp')  67.8 us
    all_gather x1, waiting for transfers between devices, per_device(): lax.all_gather(w_up, 'fsdp', axis=0, tiled=True)  60.3 us
    unnamed x227, local copies, waits for them, and re-layouts  60 us
    all_gather x1, waiting for transfers between devices, per_device(): lax.all_gather(w_down, 'fsdp', axis=1, tiled=True)  59.6 us
    all_gather x1, waiting for transfers between devices, per_device(): lax.all_gather(w_gate, 'fsdp', axis=0, tiled=True)  59.4 us
    all_gather x1, waiting for transfers between devices, per_device(): lax.all_gather(w_in, 'fsdp', axis=0, tiled=True)  50 us
  transfers between devices with their start and end apart: 8, of which 6 were waited for; matrix products, arithmetic and copies ran while one was open for 3% of the time, Pallas kernels for 0%

commit v1 on v0

--- a/solution.py
+++ b/solution.py
@@ -1,6 +1,8 @@
 import jax
 import jax.numpy as jnp
 from jax import lax
+from jax.experimental import pallas as pl
+from jax.experimental.pallas import tpu as pltpu
 from jax.sharding import PartitionSpec as P
 
 FF = 2048
@@ -109,11 +111,415 @@
     )
 
 
-def grad_block(left_full, right_rows, gain_grad, right_back, back_full):
-    return jnp.concatenate(
-        [outer_sum(left_full, right_rows), gain_grad[:, None], outer_sum(back_full, right_back)],
-        axis=1,
-    )
+MESH = pl.DeviceIdType.MESH
+IN_PAD = 3456
+PROJ = IN_PAD + QD + 2 * KD
+GATHER_CHUNKS = ((0, 0, 2176), (0, 2176, 2176), (1, 0, 2048), (2, 0, 2048), (2, 2048, 2048), (3, 0, 2048))
+REDUCE_CHUNKS = ((3, 0, 2048), (2, 0, 2048), (2, 2048, 2048), (1, 0, 2048), (0, 0, 2176), (0, 2176, 2048))
+
+
+def place_of(me):
+    return me // 8, (me // 4) % 2, (me // 2) % 2, me % 2
+
+
+def index_of(z, y, x, core):
+    return ((z * 2 + y) * 2 + x) * 2 + core
+
+
+def enter(depth, z, y, x, core):
+    barrier = pltpu.get_barrier_semaphore()
+    partners = [
+        index_of(z, y, x, 1 - core),
+        index_of(z, y, 1 - x, core),
+        index_of(z, 1 - y, x, core),
+    ] + [index_of((z + j) % depth, y, x, core) for j in range(1, depth)]
+    for partner in partners:
+        pl.semaphore_signal(barrier, inc=1, device_id=(partner,), device_id_type=MESH)
+    pl.semaphore_wait(barrier, len(partners))
+
+
+def gather_kernel(depth, *refs):
+    count = len(GATHER_CHUNKS)
+    shards, fulls = refs[:4], refs[4:8]
+    own_sem, z_send, z_recv, p_send, p_recv, c_send, c_recv = refs[8:]
+    z, y, x, core = place_of(lax.axis_index("fsdp"))
+    sibling = index_of(z, y, x, 1 - core)
+    enter(depth, z, y, x, core)
+
+    def remote(src, dst, send, recv, device):
+        return pltpu.make_async_remote_copy(
+            src_ref=src,
+            dst_ref=dst,
+            send_sem=send,
+            recv_sem=recv,
+            device_id=(device,),
+            device_id_type=MESH,
+        )
+
+    own_copies, z_copies = [], []
+    for c, (which, first, width) in enumerate(GATHER_CHUNKS):
+        cols = pl.ds(first, width)
+        mine = shards[which].at[:, cols]
+        spot = fulls[which].at[z, y, x, core, :, cols]
+        row = []
+        for j in range(1, depth):
+            copy = remote(
+                mine,
+                spot,
+                z_send.at[c, j - 1],
+                z_recv.at[c, j - 1],
+                index_of((z + j) % depth, y, x, core),
+            )
+            copy.start()
+            row.append(copy)
+        z_copies.append(row)
+        own = pltpu.make_async_copy(mine, spot, own_sem.at[c])
+        own.start()
+        own_copies.append(own)
+
+    sent = []
+
+    def region(c, ys, xs, co):
+        which, first, width = GATHER_CHUNKS[c]
+        return fulls[which].at[:, ys, xs, co, :, pl.ds(first, width)]
+
+    def to_sibling(c, step, ys, xs):
+        src = region(c, ys, xs, core)
+        copy = remote(src, src, c_send.at[c, step], c_recv.at[c, step], sibling)
+        copy.start()
+        sent.append(copy)
+
+    def step_one(c):
+        which, first, width = GATHER_CHUNKS[c]
+        for j in range(1, depth):
+            spot = fulls[which].at[(z + depth - j) % depth, y, x, core, :, pl.ds(first, width)]
+            remote(spot, spot, z_send.at[c, j - 1], z_recv.at[c, j - 1], sibling).wait_recv()
+        own_copies[c].wait()
+        src = region(c, y, x, core)
+        other = index_of(z, y, 1 - x, core) if c % 2 == 0 else index_of(z, 1 - y, x, core)
+        copy = remote(src, src, p_send.at[c, 0], p_recv.at[c, 0], other)
+        copy.start()
+        sent.append(copy)
+        to_sibling(c, 0, y, x)
+
+    def step_two(c):
+        if c % 2 == 0:
+            spot = region(c, y, 1 - x, core)
+            src = region(c, y, slice(None), core)
+            other = index_of(z, 1 - y, x, core)
+        else:
+            spot = region(c, 1 - y, x, core)
+            src = region(c, slice(None), x, core)
+            other = index_of(z, y, 1 - x, core)
+        remote(spot, spot, p_send.at[c, 0], p_recv.at[c, 0], sibling).wait_recv()
+        copy = remote(src, src, p_send.at[c, 1], p_recv.at[c, 1], other)
+        copy.start()
+        sent.append(copy)
+        if c % 2 == 0:
+            to_sibling(c, 1, y, 1 - x)
+        else:
+            to_sibling(c, 1, 1 - y, x)
+
+    def step_three(c):
+        if c % 2 == 0:
+            ys, xs = 1 - y, slice(None)
+        else:
+            ys, xs = slice(None), 1 - x
+        spot = region(c, ys, xs, core)
+        remote(spot, spot, p_send.at[c, 1], p_recv.at[c, 1], sibling).wait_recv()
+        to_sibling(c, 2, ys, xs)
+
+    for t in range(count + 2):
+        if t < count:
+            step_one(t)
+        if 0 <= t - 1 < count:
+            step_two(t - 1)
+        if 0 <= t - 2 < count:
+            step_three(t - 2)
+    for c in range(count):
+        if c % 2 == 0:
+            parts = ((y, x), (y, 1 - x), (1 - y, slice(None)))
+        else:
+            parts = ((y, x), (1 - y, x), (slice(None), 1 - x))
+        for step, (ys, xs) in enumerate(parts):
+            spot = region(c, ys, xs, 1 - core)
+            remote(spot, spot, c_send.at[c, step], c_recv.at[c, step], sibling).wait_recv()
+    for row in z_copies:
+        for copy in row:
+            copy.wait_send()
+    for copy in sent:
+        copy.wait_send()
+
+
+def gather_fast(shards, n):
+    depth = n // 8
+    rows = shards[0].shape[0]
+    count = len(GATHER_CHUNKS)
+    anywhere = pl.BlockSpec(memory_space=pl.ANY)
+    dma = pltpu.SemaphoreType.DMA
+    fulls = pl.pallas_call(
+        lambda *refs: gather_kernel(depth, *refs),
+        out_shape=tuple(
+            jax.ShapeDtypeStruct((depth, 2, 2, 2, rows, s.shape[1]), s.dtype) for s in shards
+        ),
+        in_specs=[anywhere] * 4,
+        out_specs=(anywhere,) * 4,
+        scratch_shapes=[
+            dma((count,)),
+            dma((count, depth - 1)),
+            dma((count, depth - 1)),
+            dma((count, 2)),
+            dma((count, 2)),
+            dma((count, 3)),
+            dma((count, 3)),
+        ],
+        compiler_params=pltpu.CompilerParams(collective_id=0, has_side_effects=True),
+        name="gather_weights",
+    )(*shards)
+    return tuple(f.reshape(n * rows, f.shape[-1]) for f in fulls)
+
+
+def reduce_kernel(depth, *refs):
+    count = len(REDUCE_CHUNKS)
+    grads, small = refs[:4], refs[4]
+    outs, small_out = refs[5:9], refs[9]
+    rest = list(refs[10:])
+    held = rest[:count]
+    c_buf = rest[count : 2 * count]
+    one_buf = rest[2 * count : 3 * count]
+    two_buf = rest[3 * count : 4 * count]
+    z_buf = rest[4 * count : 5 * count]
+    (s_cur, s_buf, s_z, own_sem, c_send, c_recv, p_send, p_recv, z_send, z_recv,
+     s_send, s_recv, sz_send, sz_recv) = rest[5 * count :]
+    z, y, x, core = place_of(lax.axis_index("fsdp"))
+    sibling = index_of(z, y, x, 1 - core)
+    beside_x = index_of(z, y, 1 - x, core)
+    beside_y = index_of(z, 1 - y, x, core)
+    enter(depth, z, y, x, core)
+
+    def remote(src, dst, send, recv, device):
+        return pltpu.make_async_remote_copy(
+            src_ref=src,
+            dst_ref=dst,
+            send_sem=send,
+            recv_sem=recv,
+            device_id=(device,),
+            device_id_type=MESH,
+        )
+
+    core_copies, own_copies, sent = [], [], []
+    for c, (which, first, width) in enumerate(REDUCE_CHUNKS):
+        cols = pl.ds(first, width)
+        copy = remote(
+            grads[which].at[:, :, :, 1 - core, :, cols],
+            c_buf[c],
+            c_send.at[c],
+            c_recv.at[c],
+            sibling,
+        )
+        copy.start()
+        core_copies.append(copy)
+        own = pltpu.make_async_copy(
+            grads[which].at[:, :, :, core, :, cols], held[c], own_sem.at[c]
+        )
+        own.start()
+        own_copies.append(own)
+
+    def summed(first, second):
+        return (first.astype(jnp.float32) + second.astype(jnp.float32)).astype(jnp.bfloat16)
+
+    def step_core(c):
+        own_copies[c].wait()
+        core_copies[c].wait_recv()
+
+        def add(i, carry):
+            a, b, d = i // 4, (i // 2) % 2, i % 2
+            held[c][a, b, d] = summed(held[c][a, b, d], c_buf[c][a, b, d])
+            return carry
+
+        lax.fori_loop(0, depth * 4, add, 0)
+        if c % 2 == 0:
+            copy = remote(
+                held[c].at[:, 1 - y], one_buf[c], p_send.at[c, 0], p_recv.at[c, 0], beside_y
+            )
+        else:
+            copy = remote(
+                held[c].at[:, :, 1 - x], one_buf[c], p_send.at[c, 0], p_recv.at[c, 0], beside_x
+            )
+        copy.start()
+        sent.append(copy)
+
+    def step_one(c):
+        remote(one_buf[c], one_buf[c], p_send.at[c, 0], p_recv.at[c, 0], sibling).wait_recv()
+
+        def add(i, carry):
+            a, b = i // 2, i % 2
+            if c % 2 == 0:
+                held[c][a, y, b] = summed(held[c][a, y, b], one_buf[c][a, b])
+            else:
+                held[c][a, b, x] = summed(held[c][a, b, x], one_buf[c][a, b])
+            return carry
+
+        lax.fori_loop(0, depth * 2, add, 0)
+        if c % 2 == 0:
+            src, other = held[c].at[:, y, 1 - x], beside_x
+        else:
+            src, other = held[c].at[:, 1 - y, x], beside_y
+        copy = remote(src, two_buf[c], p_send.at[c, 1], p_recv.at[c, 1], other)
+        copy.start()
+        sent.append(copy)
+
+    def step_two(c):
+        remote(two_buf[c], two_buf[c], p_send.at[c, 1], p_recv.at[c, 1], sibling).wait_recv()
+
+        def add(a, carry):
+            held[c][a, y, x] = summed(held[c][a, y, x], two_buf[c][a])
+            return carry
+
+        lax.fori_loop(0, depth, add, 0)
+        for j in range(1, depth):
+            to = (z + j) % depth
+            copy = remote(
+                held[c].at[to, y, x],
+                z_buf[c].at[j - 1],
+                z_send.at[c, j - 1],
+                z_recv.at[c, j - 1],
+                index_of(to, y, x, core),
+            )
+            copy.start()
+            sent.append(copy)
+
+    def step_z(c):
+        which, first, width = REDUCE_CHUNKS[c]
+        total = held[c][z, y, x].astype(jnp.float32)
+        for j in range(1, depth):
+            spot = z_buf[c].at[j - 1]
+            remote(spot, spot, z_send.at[c, j - 1], z_recv.at[c, j - 1], sibling).wait_recv()
+            total = total + z_buf[c][j - 1].astype(jnp.float32)
+        outs[which][:, first : first + width] = total
+
+    small_sent = []
+
+    def small_start(step):
+        if step == 0:
+            s_cur[...] = small[...]
+        if step < 3:
+            copy = remote(
+                s_cur,
+                s_buf.at[step],
+                s_send.at[step],
+                s_recv.at[step],
+                (sibling, beside_x, beside_y)[step],
+            )
+            copy.start()
+            small_sent.append(copy)
+        else:
+            s_z[z] = s_cur[...]
+            for j in range(1, depth):
+                copy = remote(
+                    s_cur,
+                    s_z.at[z],
+                    sz_send.at[j - 1],
+                    sz_recv.at[j - 1],
+                    index_of((z + j) % depth, y, x, core),
+                )
+                copy.start()
+                sent.append(copy)
+
+    def small_end(step):
+        if step < 3:
+            small_sent[step].wait()
+            s_cur[...] = s_cur[...] + s_buf[step]
+        else:
+            for j in range(1, depth):
+                spot = s_z.at[(z + depth - j) % depth]
+                remote(spot, spot, sz_send.at[j - 1], sz_recv.at[j - 1], sibling).wait_recv()
+            total = s_z[0]
+            for a in range(1, depth):
+                total = total + s_z[a]
+            small_out[...] = total
+
+    small_start(0)
+    for t in range(count + 3):
+        if t < count:
+            step_core(t)
+        if 0 <= t - 1 < count:
+            step_one(t - 1)
+        if 0 <= t - 2 < count:
+            step_two(t - 2)
+        if 0 <= t - 3 < count:
+            step_z(t - 3)
+        if t < 4:
+            small_end(t)
+        if t < 3:
+            small_start(t + 1)
+    for copy in core_copies:
+        copy.wait_send()
+    for copy in sent:
+        copy.wait_send()
+
+
+def reduce_fast(grads, small, n):
+    depth = n // 8
+    rows = grads[0].shape[0] // n
+    count = len(REDUCE_CHUNKS)
+    anywhere = pl.BlockSpec(memory_space=pl.ANY)
+    vmem = pl.BlockSpec(memory_space=pltpu.VMEM)
+    dma = pltpu.SemaphoreType.DMA
+    blocks = [g.reshape(depth, 2, 2, 2, rows, g.shape[1]) for g in grads]
+    widths = [width for (_, _, width) in REDUCE_CHUNKS]
+
+    def buffers(*lead):
+        return [pltpu.VMEM(lead + (rows, width), jnp.bfloat16) for width in widths]
+
+    return pl.pallas_call(
+        lambda *refs: reduce_kernel(depth, *refs),
+        out_shape=tuple(jax.ShapeDtypeStruct((rows, g.shape[1]), jnp.float32) for g in grads)
+        + (jax.ShapeDtypeStruct(small.shape, jnp.float32),),
+        in_specs=[anywhere] * 4 + [vmem],
+        out_specs=(vmem,) * 5,
+        scratch_shapes=buffers(depth, 2, 2)
+        + buffers(depth, 2, 2)
+        + buffers(depth, 2)
+        + buffers(depth)
+        + buffers(depth - 1)
+        + [
+            pltpu.VMEM(small.shape, jnp.float32),
+            pltpu.VMEM((3,) + small.shape, jnp.float32),
+            pltpu.VMEM((depth,) + small.shape, jnp.float32),
+            dma((count,)),
+            dma((count,)),
+            dma((count,)),
+            dma((count, 2)),
+            dma((count, 2)),
+            dma((count, depth - 1)),
+            dma((count, depth - 1)),
+            dma((3,)),
+            dma((3,)),
+            dma((depth - 1,)),
+            dma((depth - 1,)),
+        ],
+        compiler_params=pltpu.CompilerParams(
+            collective_id=1, has_side_effects=True, vmem_limit_bytes=52 * 1024 * 1024
+        ),
+        name="reduce_grads",
+    )(*blocks, small)
+
+
+def gather_weights(shards, n):
+    if n == 32:
+        return gather_fast(shards, n)
+    return tuple(lax.all_gather(s, "fsdp", axis=0, tiled=True) for s in shards)
+
+
+def reduce_grads(grads, small, n):
+    if n == 32:
+        return reduce_fast(grads, small, n)
+    summed = [
+        lax.psum_scatter(g.astype(jnp.float32), "fsdp", scatter_dimension=0, tiled=True)
+        for g in grads
+    ]
+    return (*summed, lax.psum(small, "fsdp"))
 
 
 def per_device(
@@ -137,32 +543,33 @@
     a_log,
     d_skip,
 ):
-    gathered = (
-        lax.all_gather(w_in, "fsdp", axis=0, tiled=True),
-        lax.all_gather(w_q, "fsdp", axis=0, tiled=True),
-        lax.all_gather(w_k, "fsdp", axis=0, tiled=True),
-        lax.all_gather(w_v, "fsdp", axis=0, tiled=True),
-        lax.all_gather(w_gate, "fsdp", axis=0, tiled=True),
-        lax.all_gather(w_up, "fsdp", axis=0, tiled=True),
-        lax.all_gather(gain_a, "fsdp", axis=0, tiled=True),
-        lax.all_gather(gain_b, "fsdp", axis=0, tiled=True),
-        lax.all_gather(w_o, "fsdp", axis=1, tiled=True),
-        lax.all_gather(w_out, "fsdp", axis=1, tiled=True),
-        lax.all_gather(w_down, "fsdp", axis=1, tiled=True),
-    )
-    (
-        full_in,
-        full_q,
-        full_k,
-        full_v,
-        full_gate,
-        full_up,
-        full_ga,
-        full_gb,
-        full_o,
-        full_out,
-        full_down,
-    ) = gathered
+    n = lax.axis_size("fsdp")
+    rows = w_in.shape[0]
+
+    def blank(columns):
+        return jnp.zeros((rows, columns), jnp.bfloat16)
+
+    shards = (
+        jnp.concatenate(
+            [
+                w_in,
+                blank(IN_PAD - DIN),
+                w_q,
+                w_k,
+                w_v,
+                gain_a[:, None],
+                gain_b[:, None],
+                blank(126),
+            ],
+            axis=1,
+        ),
+        jnp.concatenate([w_o.T, w_out.T], axis=1),
+        jnp.concatenate([w_gate, w_up], axis=1),
+        w_down.T,
+    )
+    full_proj, full_mixed, full_glu, full_down = gather_weights(shards, n)
+    full_ga = full_proj[:, PROJ]
+    full_gb = full_proj[:, PROJ + 1]
     row_count = tokens.shape[0]
     segment, position = segment_layout(lengths[0], row_count)
     places = jnp.arange(row_count)
@@ -170,10 +577,11 @@
     resid_in = tokens.astype(jnp.float32)
     normed_f, norm_back_a = jax.vjp(rms_scaled, resid_in, full_ga.astype(jnp.float32))
     normed = normed_f.astype(jnp.bfloat16)
-    zxd = forward_prod(normed, full_in)
-    q_raw = forward_prod(normed, full_q)
-    k_raw = forward_prod(normed, full_k)
-    v_low = forward_prod(normed, full_v).astype(jnp.bfloat16)
+    projected = forward_prod(normed, full_proj)
+    zxd = projected[:, :DIN]
+    q_raw = projected[:, IN_PAD : IN_PAD + QD]
+    k_raw = projected[:, IN_PAD + QD : IN_PAD + QD + KD]
+    v_low = projected[:, IN_PAD + QD + KD : PROJ].astype(jnp.bfloat16)
     z_gate = zxd[:, :DSSM]
     xbc_in = zxd[:, DSSM : DSSM + CONV]
     dt_raw = zxd[:, DSSM + CONV :]
@@ -226,40 +634,29 @@
         preferred_element_type=jnp.float32,
     )
     context = attended.astype(jnp.bfloat16).reshape(row_count, QD)
-    attn_out = forward_prod(context, full_o)
-    mamba_out = forward_prod(gated_low, full_out)
-    mid_sum = resid_in + attn_out + mamba_out
+    mixed_outs = jnp.concatenate([context, gated_low], axis=1)
+    mid_sum = resid_in + back_prod(mixed_outs, full_mixed)
     normed_bf, norm_back_b = jax.vjp(rms_scaled, mid_sum, full_gb.astype(jnp.float32))
     normed_b = normed_bf.astype(jnp.bfloat16)
-    gate_pre = forward_prod(normed_b, full_gate)
-    upward = forward_prod(normed_b, full_up)
+    glu_pre = forward_prod(normed_b, full_glu)
+    gate_pre = glu_pre[:, :FF]
+    upward = glu_pre[:, FF:]
     hidden_f, glu_back = jax.vjp(swiglu, gate_pre, upward)
     hidden = hidden_f.astype(jnp.bfloat16)
-    result = (mid_sum + forward_prod(hidden, full_down)).astype(jnp.bfloat16)
-    regathered = (
-        lax.all_gather(w_in, "fsdp", axis=0, tiled=True),
-        lax.all_gather(w_q, "fsdp", axis=0, tiled=True),
-        lax.all_gather(w_k, "fsdp", axis=0, tiled=True),
-        lax.all_gather(w_v, "fsdp", axis=0, tiled=True),
-        lax.all_gather(w_gate, "fsdp", axis=0, tiled=True),
-        lax.all_gather(w_up, "fsdp", axis=0, tiled=True),
-        lax.all_gather(w_o, "fsdp", axis=1, tiled=True),
-        lax.all_gather(w_out, "fsdp", axis=1, tiled=True),
-        lax.all_gather(w_down, "fsdp", axis=1, tiled=True),
-    )
-    back_in, back_q, back_k, back_v, back_gate, back_up, back_o, back_out, back_down = regathered
+    result = (mid_sum + back_prod(hidden, full_down)).astype(jnp.bfloat16)
     grad_top = cotangent.astype(jnp.float32)
-    d_hidden = back_prod(cotangent, back_down)
+    d_hidden = forward_prod(cotangent, full_down)
     d_gate_f, d_up_f = glu_back(d_hidden)
     d_gate = d_gate_f.astype(jnp.bfloat16)
     d_up = d_up_f.astype(jnp.bfloat16)
     d_glu = jnp.concatenate([d_gate, d_up], axis=1)
-    d_normed_b = back_prod(d_gate, back_gate) + back_prod(d_up, back_up)
+    d_normed_b = back_prod(d_glu, full_glu)
     d_mid_norm, g_gain_b = norm_back_b(d_normed_b)
     d_mid = grad_top + d_mid_norm
     d_branch = d_mid.astype(jnp.bfloat16)
-    d_context = back_prod(d_branch, back_o)
-    d_gated = back_prod(d_branch, back_out)
+    d_mixed = forward_prod(d_branch, full_mixed)
+    d_context = d_mixed[:, :QD]
+    d_gated = d_mixed[:, QD:]
     d_att_low = d_context.reshape(row_count, KV_HEADS, group_size, HEAD_DIM).astype(jnp.bfloat16)
     masked_again = masked_scores()
     prob_again = jnp.exp(masked_again - row_peak) / row_total
@@ -295,46 +692,54 @@
         (d_x_heads, d_b_state, d_c_state, d_step, d_decay)
     )
     d_zxd = jnp.concatenate([d_z, d_xbc, d_dt_raw], axis=1).astype(jnp.bfloat16)
-    d_proj = jnp.concatenate([d_zxd, d_q_low, d_k_low, d_v_low], axis=1)
-    d_normed = (
-        back_prod(d_zxd, back_in)
-        + back_prod(d_q_low, back_q)
-        + back_prod(d_k_low, back_k)
-        + back_prod(d_v_low, back_v)
-    )
+    d_proj = jnp.concatenate(
+        [d_zxd, jnp.zeros((row_count, IN_PAD - DIN), jnp.bfloat16), d_q_low, d_k_low, d_v_low],
+        axis=1,
+    )
+    d_normed = back_prod(d_proj, full_proj[:, :PROJ])
     d_resid, g_gain_a = norm_back_a(d_normed)
     d_tokens = (d_mid + d_resid).astype(jnp.bfloat16)
-    mixed_outs = jnp.concatenate([context, gated_low], axis=1)
-    sum_conv_w, sum_conv_b, sum_dt_bias, sum_a_log, sum_skip = lax.psum(
-        (g_conv_w, g_conv_b, g_dt_bias, g_a_log, g_skip), "fsdp"
-    )
-    all_rows = lax.psum_scatter(
-        jnp.concatenate(
-            [
-                grad_block(normed_b, d_glu, g_gain_b, hidden, cotangent),
-                grad_block(normed, d_proj, g_gain_a, mixed_outs, d_branch),
-            ],
-            axis=1,
-        ),
-        "fsdp",
-        scatter_dimension=0,
-        tiled=True,
-    )
-    ffn_cols = 3 * FF + 1
-    ffn_rows = all_rows[:, :ffn_cols]
-    mixer_rows = all_rows[:, ffn_cols:]
-    sum_gate = ffn_rows[:, :FF]
-    sum_up = ffn_rows[:, FF : 2 * FF]
-    sum_gain_b = ffn_rows[:, 2 * FF]
-    sum_down = ffn_rows[:, 2 * FF + 1 :].T
-    proj_cols = DIN + QD + 2 * KD
-    sum_in = mixer_rows[:, :DIN]
-    sum_q = mixer_rows[:, DIN : DIN + QD]
-    sum_k = mixer_rows[:, DIN + QD : DIN + QD + KD]
-    sum_v = mixer_rows[:, DIN + QD + KD : proj_cols]
-    sum_gain_a = mixer_rows[:, proj_cols]
-    sum_o = mixer_rows[:, proj_cols + 1 : proj_cols + 1 + QD].T
-    sum_out = mixer_rows[:, proj_cols + 1 + QD :].T
+    flat = jnp.concatenate(
+        [
+            g_gain_a,
+            g_gain_b,
+            g_conv_w.reshape(-1),
+            g_conv_b,
+            g_dt_bias,
+            g_a_log,
+            g_skip,
+        ]
+    )
+    small_rows = -(-flat.shape[0] // 1024) * 8
+    small = jnp.pad(flat, (0, small_rows * 128 - flat.shape[0])).reshape(small_rows, 128)
+    grads = (
+        outer_sum(normed, d_proj).astype(jnp.bfloat16),
+        outer_sum(d_branch, mixed_outs).astype(jnp.bfloat16),
+        outer_sum(normed_b, d_glu).astype(jnp.bfloat16),
+        outer_sum(cotangent, hidden).astype(jnp.bfloat16),
+    )
+    proj_rows, mixed_rows, glu_rows, down_rows, small_sum = reduce_grads(grads, small, n)
+    sum_in = proj_rows[:, :DIN]
+    sum_q = proj_rows[:, IN_PAD : IN_PAD + QD]
+    sum_k = proj_rows[:, IN_PAD + QD : IN_PAD + QD + KD]
+    sum_v = proj_rows[:, IN_PAD + QD + KD :]
+    sum_o = mixed_rows[:, :QD].T
+    sum_out = mixed_rows[:, QD:].T
+    sum_gate = glu_rows[:, :FF]
+    sum_up = glu_rows[:, FF:]
+    sum_down = down_rows.T
+    width = n * rows
+    flat_sum = small_sum.reshape(-1)
+    here = lax.axis_index("fsdp") * rows
+    sum_gain_a = lax.dynamic_slice(flat_sum, (here,), (rows,))
+    sum_gain_b = lax.dynamic_slice(flat_sum, (width + here,), (rows,))
+    start = 2 * width
+    pieces = []
+    for size in (4 * CONV, CONV, 24, 24, 24):
+        pieces.append(flat_sum[start : start + size])
+        start += size
+    sum_conv_w, sum_conv_b, sum_dt_bias, sum_a_log, sum_skip = pieces
+    sum_conv_w = sum_conv_w.reshape(4, CONV)
     return (
         result,
         d_tokens,

time: 1270 us -> 451 us (0.36)
  waiting for transfers between devices: 746 us -> 0 us
  Pallas kernels: 0 us -> 293 us
  blocking collectives: 189 us -> 0 us
  local copies, waits for them, and re-layouts: 200 us -> 43.6 us
  between operations: 16 us -> 1.71 us
    unnamed x9 -> x0, waiting for transfers between devices: 472 us -> none
    pallas_call x0 -> x2, Pallas kernels: none -> 293 us  [the longest x1 147 us: reduce_fast(): pl.pallas_call(lambda *refs: reduce_kernel(depth, *refs), out_shape=tuple...]
    all_gather x7 -> x0, waiting for transfers between devices: 275 us -> none  [the longest x1 60.3 us: per_device(): lax.all_gather(w_up, 'fsdp', axis=0, tiled=True)]
    concatenate x2 -> x3, local copies, waits for them, and re-layouts: 124 us -> 4.26 us  [the longest x1 2.42 us: per_device(): jnp.concatenate([d_zxd, jnp.zeros((row_count, IN_PAD - DIN), jnp.bfloat16...]
    all_gather x2 -> x0, blocking collectives: 80.4 us -> none  [the longest x1 42.7 us: per_device(): lax.all_gather(w_k, 'fsdp', axis=0, tiled=True)]
    psum x1 -> x0, blocking collectives: 67.8 us -> none  [per_device(): lax.psum((g_conv_w, g_conv_b, g_dt_bias, g_a_log, g_skip), 'fsdp')]
    unnamed x227 -> x141, local copies, waits for them, and re-layouts: 60 us -> 3.91 us
    unnamed x1 -> x0, blocking collectives: 40.6 us -> none
  transfers between devices with their start and end apart: 8 -> 0, of which waited for: 6 -> 0; matrix products, arithmetic and copies ran while one was open for 3% -> 0% of each run, Pallas kernels for 0% -> 0%
where the time goes in v1:
time: 451 us; the launch traced here: 446 us
  Pallas kernels  293 us (65%)
  matrix products  74.2 us (16%)
  local copies, waits for them, and re-layouts  43.6 us (10%)
  other arithmetic  33.2 us (7%)
    pallas_call x1, Pallas kernels, reduce_fast(): pl.pallas_call(lambda *refs: reduce_kernel(depth, *refs), out_shape=tuple...  147 us
    pallas_call x1, Pallas kernels, gather_fast(): pl.pallas_call(lambda *refs: gather_kernel(depth, *refs), out_shape=tuple...  146 us
    dot_general x4, matrix products, back_prod(): lax.dot_general(grad_rows, weight, (((1,), (1,)), ((), ())), preferred_el...  23 us
    dot_general x5, matrix products, outer_sum(): lax.dot_general(left_rows, right_rows, (((0,), (0,)), ((), ())), preferre...  20.7 us
    dot_general x4, matrix products, forward_prod(): return jnp.dot(rows_in, weight, preferred_element_type=jnp.float32)  12.7 us

profile of v1, /device:TPU:1, one launch (start us, length us, event | category | flops | bytes accessed | tf_op | source)
XLA Modules:
  0.0 445.7 jit_solution(13219649986053074784)
XLA Ops:
  7.2 146.4 %gather_weights.1 = (bf16[4,2,2,2,32,4352]{5,4,3,2,1,0:T(8,128)(2,1)}, bf16[4,2,2,2,32,2048]{5,4,3,2,1,0:T(8,128)(2,1)}, bf16[4,2,2,2,32,4096]{5,4,3,2,1,0:T(8,128)(2,1)}, bf16[4,2,2,2,32,2048]{5,4,3,2,1,0:T(8,128)(2,1)}) custom-call(bf16[32,4352]{1,0:T(8,128)(2,1)} %concatenate.37.refs_0_, bf16[32,2048]{1,0:T(8,128)(2,1)} %pad_maximum_fusion.7.refs_1_, ...), custom_call_target="tpu_custom_call" | custom-call | tf_op jit(solution)/shard_map/gather_weights/pallas_call | solution.py:260
  155.7 4.9 %fusion.60 = f32[128,4352]{1,0:T(8,128)S(1)} fusion(bf16[1024,4352]{1,0:T(8,128)(2,1)} %bitcast.156, bf16[128,1024]{1,0:T(8,128)(2,1)S(1)} %copy-done.1, f32[1024]{0:T(1024)S(1)} %bitcast.176, f32[128]{0:T(128)S(1)} %fusion.77), kind=kOutput, calls=%fused_computation.136 | convolution fusion | flops 1141374976 | bytes 11407872 | tf_op jit(solution)/shard_map/dot_general | solution.py:99
  169.0 2.3 copy.132
  177.9 3.1 fusion.3
  181.0 2.3 copy.136
  184.7 4.0 multiply_reduce_fusion.10
  189.4 4.9 %fusion.92 = f32[128,4096]{1,0:T(8,128)S(1)} fusion(bf16[1024,4096]{1,0:T(8,128)(2,1)} %bitcast.149, f32[128,1024]{1,0:T(8,128)S(1)} %get-tuple-element.99, f32[1024]{0:T(1024)S(1)} %bitcast.172, f32[128]{0:T(128)} %fusion.78), kind=kOutput, calls=%fused_computation.207 | convolution fusion | flops 1074135040 | bytes 11014656 | tf_op jit(solution)/shard_map/dot_general | solution.py:99
  194.3 2.2 fusion.14
  196.5 7.4 %multiply_reduce_fusion.7 = (f32[1024]{0:T(1024)}, f32[128]{0:T(128)S(1)}, f32[128,1024]{1,0:T(8,128)S(1)}) fusion(f32[128,1024]{1,0:T(8,128)S(1)} %get-tuple-element.99, f32[128]{0:T(128)S(1)} %copy-done.45, f32[1024]{0:T(1024)S(1)} %bitcast.173, bf16[1024,4096]{1,0:T(8,128)(2,1)} %bitcast.150, bf16[128,2048]{1,0:T(8,128)(2,1)S(1)} %get-tuple-element.66, ...), kind=kOutput, calls=%fused_computation.105 | convolution fusion | flops 1076624256 | bytes 10494976 | tf_op jit(solution)/shard_map/dot_general | solution.py:109
  207.6 2.3 copy.141
  210.0 3.4 fusion.17
  216.5 2.2 multiply_reduce_fusion.6
  218.7 2.3 copy.142
  221.0 4.9 %multiply_reduce_fusion.3 = (f32[1792]{0:T(1024)S(1)}, f32[1792]{0:T(1024)S(1)}, f32[1792]{0:T(1024)S(1)}, f32[1792]{0:T(1024)}, f32[1792]{0:T(1024)S(1)}, /*index=5*/f32[128,1792]{1,0:T(8,128)}) fusion(f32[128,1792]{1,0:T(8,128)} %copy-done.2, f32[128]{0:T(128)} %copy-done.56, f32[128]{0:T(128)} %copy-done.55, f32[128]{0:T(128)} %copy-done.54, ...), kind=kLoop, calls=%fused_computation.62 | loop fusion | flops 5266688 | bytes 4624896 | tf_op jit(solution)/shard_map/transpose(jvp())/reduce_sum | solution.py:67
  247.2 2.6 reduce_window_sum.30
  251.2 2.2 fusion.93
  256.1 2.4 concatenate.46
  258.6 7.2 %fusion.44 = (f32[1024]{0:T(1024)S(1)}, f32[128]{0:T(128)S(1)}, f32[128,1024]{1,0:T(8,128)}) fusion(bf16[128,1024]{1,0:T(8,128)(2,1)S(1)} %copy-done.1, f32[128]{0:T(128)S(1)} %copy-done.50, f32[1024]{0:T(1024)S(1)} %bitcast.177, bf16[128,4224]{1,0:T(8,128)(2,1)S(1)} %concatenate.46, bf16[1024,4352]{1,0:T(8,128)(2,1)} %bitcast.157), kind=kOutput, calls=%fused_computation.98 | convolution fusion | flops 1108212608 | bytes 10527744 | tf_op jit(solution)/shard_map/dot_general | solution.py:109
  266.2 6.8 %convolution_convert_fusion.1 = bf16[1024,4096]{1,0:T(8,128)(2,1)} fusion(bf16[128,2048]{1,0:T(8,128)(2,1)} %copy-done.15, bf16[128,2048]{1,0:T(8,128)(2,1)S(1)} %copy-done.14, f32[128,1024]{1,0:T(8,128)S(1)} %get-tuple-element.99, f32[1024]{0:T(1024)S(1)} %bitcast.175, f32[128]{0:T(128)S(1)} %copy-done.46), kind=kOutput, calls=%fused_computation.4 | convolution fusion | flops 1080426496 | bytes 9966080 | tf_op jit(solution)/shard_map/dot_general | solution.py:103
  273.0 3.3 convolution_convert_fusion.3
  276.3 5.8 %convolution_convert_fusion = bf16[1024,4224]{1,0:T(8,128)(2,1)} fusion(bf16[128,4224]{1,0:T(8,128)(2,1)S(1)} %concatenate.46, bf16[128,1024]{1,0:T(8,128)(2,1)S(1)} %copy-done.1, f32[1024]{0:T(1024)S(1)} %bitcast.178, f32[128]{0:T(128)S(1)} %copy-done.50), kind=kOutput, calls=%fused_computation.1 | convolution fusion | flops 1112145920 | bytes 9998848 | tf_op jit(solution)/shard_map/dot_general | solution.py:103
  282.1 3.3 convolution_convert_fusion.2
  285.4 146.6 %reduce_grads.1 = (f32[32,4224]{1,0:T(8,128)S(1)}, f32[32,2048]{1,0:T(8,128)S(1)}, f32[32,4096]{1,0:T(8,128)S(1)}, f32[32,2048]{1,0:T(8,128)S(1)}, f32[88,128]{1,0:T(8,128)S(1)}) custom-call(bf16[4,2,2,2,32,4224]{5,4,3,2,1,0:T(8,128)(2,1)} %bitcast.151, bf16[4,2,2,2,32,2048]{5,4,3,2,1,0:T(8,128)(2,1)} %bitcast.153, ...), custom_call_target="tpu_custom_call" | custom-call | tf_op jit(solution)/shard_map/reduce_grads/pallas_call | solution.py:475
  440.6 4.4 fusion.8
  (234 shorter events, 66.9 us)
Async XLA Ops:
  0.7 154.3 %copy-start.1 = (bf16[128,1024]{1,0:T(8,128)(2,1)S(1)}, bf16[128,1024]{1,0:T(8,128)(2,1)}, u32[]{:S(2)}) copy-start(bf16[128,1024]{1,0:T(8,128)(2,1)} %param.19) | copy-start | bytes 786436
  167.0 14.0 %copy-start.22 = (bf16[128,1792]{1,0:T(8,128)(2,1)}, bf16[128,1792]{1,0:T(8,128)(2,1)S(1)}, u32[]{:S(2)}) copy-start(bf16[128,1792]{1,0:T(8,128)(2,1)S(1)} %get-tuple-element.57) | copy-start | bytes 1376260
  171.3 12.0 %copy-start.58 = (f32[24]{0:T(128)}, f32[24]{0:T(128)S(1)}, u32[]{:S(2)}) copy-start(f32[24]{0:T(128)S(1)} %exponential_negate_fusion) | copy-start | bytes 292
  172.6 10.7 %copy-start.23 = (f32[128,24]{1,0:T(8,128)}, f32[128,24]{1,0:T(8,128)S(1)}, u32[]{:S(2)}) copy-start(f32[128,24]{1,0:T(8,128)S(1)} %get-tuple-element.61) | copy-start | bytes 36868
  196.5 7.4 %copy-start.13 = (bf16[128,2048]{1,0:T(8,128)(2,1)}, bf16[128,2048]{1,0:T(8,128)(2,1)S(1)}, u32[]{:S(2)}) copy-start(bf16[128,2048]{1,0:T(8,128)(2,1)S(1)} %get-tuple-element.65) | copy-start | bytes 1572868
  196.5 7.4 %copy-start.15 = (bf16[128,2048]{1,0:T(8,128)(2,1)}, bf16[128,2048]{1,0:T(8,128)(2,1)S(1)}, u32[]{:S(2)}) copy-start(bf16[128,2048]{1,0:T(8,128)(2,1)S(1)} %get-tuple-element.66) | copy-start | bytes 1572868
  196.5 7.4 %copy-start.64 = (f32[128]{0:T(128)S(1)}, f32[128]{0:T(128)}, u32[]{:S(2)}) copy-start(f32[128]{0:T(128)} %copy-done.63) | copy-start | bytes 1540
  196.5 7.6 %copy-start = (bf16[4,2,2,2,32,2048]{5,4,3,2,1,0:T(8,128)(2,1)S(1)}, bf16[4,2,2,2,32,2048]{5,4,3,2,1,0:T(8,128)(2,1)}, u32[]{:S(2)}) copy-start(bf16[4,2,2,2,32,2048]{5,4,3,2,1,0:T(8,128)(2,1)} %get-tuple-element.28) | copy-start | bytes 12582916
  209.9 6.5 %copy-start.48 = (pred[128,128]{1,0:T(8,128)(4,1)S(1)}, pred[128,128]{1,0:T(8,128)(4,1)}, u32[]{:S(2)}) copy-start(pred[128,128]{1,0:T(8,128)(4,1)} %copy.133) | copy-start | bytes 49156
  209.9 6.5 %copy-start.51 = (f32[128,24]{0,1:T(8,128)S(1)}, f32[128,24]{0,1:T(8,128)}, u32[]{:S(2)}) copy-start(f32[128,24]{0,1:T(8,128)} %copy.131) | copy-start | bytes 36868
  210.0 6.5 %copy-start.52 = (f32[24,128]{1,0:T(8,128)S(1)}, f32[24,128]{1,0:T(8,128)}, u32[]{:S(2)}) copy-start(f32[24,128]{1,0:T(8,128)} %copy.134) | copy-start | bytes 36868
  210.0 6.5 %copy-start.66 = (f32[24]{0:T(128)S(1)}, f32[24]{0:T(128)}, u32[]{:S(2)}) copy-start(f32[24]{0:T(128)} %param.37) | copy-start | bytes 292
  258.5 7.3 %copy-start.62 = (f32[24]{0:T(128)S(1)}, f32[24]{0:T(128)}, u32[]{:S(2)}) copy-start(f32[24]{0:T(128)} %get-tuple-element.81) | copy-start | bytes 292
  258.6 7.3 %copy-start.68 = (f32[24]{0:T(128)S(1)}, f32[24]{0:T(128)}, u32[]{:S(2)}) copy-start(f32[24]{0:T(128)} %param.36) | copy-start | bytes 292
  258.6 7.3 %copy-start.42 = (f32[1536]{0:T(1024)S(1)}, f32[1536]{0:T(1024)}, u32[]{:S(2)}) copy-start(f32[1536]{0:T(1024)} %get-tuple-element.52) | copy-start | bytes 18436
  258.6 7.5 %copy-start.33 = (f32[7168]{0:T(1024)S(1)}, f32[7168]{0:T(1024)}, u32[]{:S(2)}) copy-start(f32[7168]{0:T(1024)} %reshape.390) | copy-start | bytes 86020
  258.6 7.5 %copy-start.41 = (f32[1792]{0:T(1024)S(1)}, f32[1792]{0:T(1024)}, u32[]{:S(2)}) copy-start(f32[1792]{0:T(1024)} %get-tuple-element.44) | copy-start | bytes 21508
  258.6 7.5 %copy-start.47 = (f32[1024]{0:T(1024)S(1)}, f32[1024]{0:T(1024)}, u32[]{:S(2)}) copy-start(f32[1024]{0:T(1024)} %get-tuple-element.42) | copy-start | bytes 12292
  258.6 7.5 %copy-start.59 = (f32[24]{0:T(128)S(1)}, f32[24]{0:T(128)}, u32[]{:S(2)}) copy-start(f32[24]{0:T(128)} %get-tuple-element.54) | copy-start | bytes 292
  258.6 7.6 %copy-start.14 = (bf16[128,2048]{1,0:T(8,128)(2,1)S(1)}, bf16[128,2048]{1,0:T(8,128)(2,1)}, u32[]{:S(2)}) copy-start(bf16[128,2048]{1,0:T(8,128)(2,1)} %copy-done.13) | copy-start | bytes 1572868
  258.6 7.5 %copy-start.46 = (f32[128]{0:T(128)S(1)}, f32[128]{0:T(128)}, u32[]{:S(2)}) copy-start(f32[128]{0:T(128)} %fusion.78) | copy-start | bytes 1540
  266.2 6.8 %copy-start.11 = (bf16[128,1536]{1,0:T(8,128)(2,1)S(1)}, bf16[128,1536]{1,0:T(8,128)(2,1)}, u32[]{:S(2)}) copy-start(bf16[128,1536]{1,0:T(8,128)(2,1)} %copy-done.10) | copy-start | bytes 1179652
  266.2 6.8 %copy-start.17 = (bf16[128,512]{1,0:T(8,128)(2,1)S(1)}, bf16[128,512]{1,0:T(8,128)(2,1)}, u32[]{:S(2)}) copy-start(bf16[128,512]{1,0:T(8,128)(2,1)} %copy.137) | copy-start | bytes 393220
  432.0 6.6 %copy-start.61 = (f32[128]{0:T(128)S(1)}, f32[128]{0:T(128)}, u32[]{:S(2)}) copy-start(f32[128]{0:T(128)} %copy-done.60) | copy-start | bytes 1540
  (45 other events, 141.1 us)

commit v2 on v1

--- a/solution.py
+++ b/solution.py
@@ -114,8 +114,9 @@
 MESH = pl.DeviceIdType.MESH
 IN_PAD = 3456
 PROJ = IN_PAD + QD + 2 * KD
-GATHER_CHUNKS = ((0, 0, 2176), (0, 2176, 2176), (1, 0, 2048), (2, 0, 2048), (2, 2048, 2048), (3, 0, 2048))
-REDUCE_CHUNKS = ((3, 0, 2048), (2, 0, 2048), (2, 2048, 2048), (1, 0, 2048), (0, 0, 2176), (0, 2176, 2048))
+GATHER_CHUNKS = ((0, 0, 1024), (1, 0, 2048), (0, 1024, 3328), (2, 0, 2048), (2, 2048, 2048), (3, 0, 2048))
+REDUCE_CHUNKS = ((3, 0, 2048), (2, 0, 2048), (2, 2048, 2048), (0, 0, 3200), (1, 0, 2048), (0, 3200, 1024))
+AHEAD = 2
 
 
 def place_of(me):
@@ -157,7 +158,9 @@
         )
 
     own_copies, z_copies = [], []
-    for c, (which, first, width) in enumerate(GATHER_CHUNKS):
+
+    def start_z(c):
+        which, first, width = GATHER_CHUNKS[c]
         cols = pl.ds(first, width)
         mine = shards[which].at[:, cols]
         spot = fulls[which].at[z, y, x, core, :, cols]
@@ -177,6 +180,9 @@
         own.start()
         own_copies.append(own)
 
+    for c in range(AHEAD):
+        start_z(c)
+
     sent = []
 
     def region(c, ys, xs, co):
@@ -195,6 +201,8 @@
             spot = fulls[which].at[(z + depth - j) % depth, y, x, core, :, pl.ds(first, width)]
             remote(spot, spot, z_send.at[c, j - 1], z_recv.at[c, j - 1], sibling).wait_recv()
         own_copies[c].wait()
+        if c + AHEAD < count:
+            start_z(c + AHEAD)
         src = region(c, y, x, core)
         other = index_of(z, y, 1 - x, core) if c % 2 == 0 else index_of(z, 1 - y, x, core)
         copy = remote(src, src, p_send.at[c, 0], p_recv.at[c, 0], other)
@@ -308,7 +316,9 @@
         )
 
     core_copies, own_copies, sent = [], [], []
-    for c, (which, first, width) in enumerate(REDUCE_CHUNKS):
+
+    def start_core(c):
+        which, first, width = REDUCE_CHUNKS[c]
         cols = pl.ds(first, width)
         copy = remote(
             grads[which].at[:, :, :, 1 - core, :, cols],
@@ -325,12 +335,17 @@
         own.start()
         own_copies.append(own)
 
+    for c in range(AHEAD):
+        start_core(c)
+
     def summed(first, second):
         return (first.astype(jnp.float32) + second.astype(jnp.float32)).astype(jnp.bfloat16)
 
     def step_core(c):
         own_copies[c].wait()
         core_copies[c].wait_recv()
+        if c + AHEAD < count:
+            start_core(c + AHEAD)
 
         def add(i, carry):
             a, b, d = i // 4, (i // 2) % 2, i % 2

time: 451 us -> 452 us (level)
  no operation moved by 1% of the time
where the time goes in v2:
time: 452 us; the launch traced here: 447 us
  Pallas kernels  294 us (65%)
  matrix products  74.2 us (16%)
  local copies, waits for them, and re-layouts  43.7 us (10%)
  other arithmetic  33.2 us (7%)
    pallas_call x1, Pallas kernels, reduce_fast(): pl.pallas_call(lambda *refs: reduce_kernel(depth, *refs), out_shape=tuple...  149 us
    pallas_call x1, Pallas kernels, gather_fast(): pl.pallas_call(lambda *refs: gather_kernel(depth, *refs), out_shape=tuple...  145 us
    dot_general x4, matrix products, back_prod(): lax.dot_general(grad_rows, weight, (((1,), (1,)), ((), ())), preferred_el...  23 us
    dot_general x5, matrix products, outer_sum(): lax.dot_general(left_rows, right_rows, (((0,), (0,)), ((), ())), preferre...  20.7 us
    dot_general x4, matrix products, forward_prod(): return jnp.dot(rows_in, weight, preferred_element_type=jnp.float32)  12.7 us

profile of v2, /device:TPU:1, one launch (start us, length us, event | category | flops | bytes accessed | tf_op | source)
XLA Modules:
  0.0 446.5 jit_solution(3451404010409589916)
XLA Ops:
  7.2 144.8 %gather_weights.1 = (bf16[4,2,2,2,32,4352]{5,4,3,2,1,0:T(8,128)(2,1)}, bf16[4,2,2,2,32,2048]{5,4,3,2,1,0:T(8,128)(2,1)}, bf16[4,2,2,2,32,4096]{5,4,3,2,1,0:T(8,128)(2,1)}, bf16[4,2,2,2,32,2048]{5,4,3,2,1,0:T(8,128)(2,1)}) custom-call(bf16[32,4352]{1,0:T(8,128)(2,1)} %concatenate.37.refs_0_, bf16[32,2048]{1,0:T(8,128)(2,1)} %pad_maximum_fusion.7.refs_1_, ...), custom_call_target="tpu_custom_call" | custom-call | tf_op jit(solution)/shard_map/gather_weights/pallas_call | solution.py:268
  154.0 4.9 %fusion.60 = f32[128,4352]{1,0:T(8,128)S(1)} fusion(bf16[1024,4352]{1,0:T(8,128)(2,1)} %bitcast.156, bf16[128,1024]{1,0:T(8,128)(2,1)S(1)} %copy-done.1, f32[1024]{0:T(1024)S(1)} %bitcast.176, f32[128]{0:T(128)S(1)} %fusion.77), kind=kOutput, calls=%fused_computation.136 | convolution fusion | flops 1141374976 | bytes 11407872 | tf_op jit(solution)/shard_map/dot_general | solution.py:99
  167.4 2.3 copy.132
  176.2 3.1 fusion.3
  179.3 2.3 copy.136
  183.0 4.0 multiply_reduce_fusion.10
  187.8 4.9 %fusion.92 = f32[128,4096]{1,0:T(8,128)S(1)} fusion(bf16[1024,4096]{1,0:T(8,128)(2,1)} %bitcast.149, f32[128,1024]{1,0:T(8,128)S(1)} %get-tuple-element.99, f32[1024]{0:T(1024)S(1)} %bitcast.172, f32[128]{0:T(128)} %fusion.78), kind=kOutput, calls=%fused_computation.207 | convolution fusion | flops 1074135040 | bytes 11014656 | tf_op jit(solution)/shard_map/dot_general | solution.py:99
  192.7 2.2 fusion.14
  194.9 7.4 %multiply_reduce_fusion.7 = (f32[1024]{0:T(1024)}, f32[128]{0:T(128)S(1)}, f32[128,1024]{1,0:T(8,128)S(1)}) fusion(f32[128,1024]{1,0:T(8,128)S(1)} %get-tuple-element.99, f32[128]{0:T(128)S(1)} %copy-done.45, f32[1024]{0:T(1024)S(1)} %bitcast.173, bf16[1024,4096]{1,0:T(8,128)(2,1)} %bitcast.150, bf16[128,2048]{1,0:T(8,128)(2,1)S(1)} %get-tuple-element.66, ...), kind=kOutput, calls=%fused_computation.105 | convolution fusion | flops 1076624256 | bytes 10494976 | tf_op jit(solution)/shard_map/dot_general | solution.py:109
  206.2 2.3 copy.141
  208.5 3.4 fusion.17
  215.0 2.2 multiply_reduce_fusion.6
  217.3 2.3 copy.142
  219.5 4.9 %multiply_reduce_fusion.3 = (f32[1792]{0:T(1024)S(1)}, f32[1792]{0:T(1024)S(1)}, f32[1792]{0:T(1024)S(1)}, f32[1792]{0:T(1024)}, f32[1792]{0:T(1024)S(1)}, /*index=5*/f32[128,1792]{1,0:T(8,128)}) fusion(f32[128,1792]{1,0:T(8,128)} %copy-done.2, f32[128]{0:T(128)} %copy-done.56, f32[128]{0:T(128)} %copy-done.55, f32[128]{0:T(128)} %copy-done.54, ...), kind=kLoop, calls=%fused_computation.62 | loop fusion | flops 5266688 | bytes 4624896 | tf_op jit(solution)/shard_map/transpose(jvp())/reduce_sum | solution.py:67
  245.7 2.6 reduce_window_sum.30
  249.7 2.2 fusion.93
  254.6 2.4 concatenate.46
  257.1 7.2 %fusion.44 = (f32[1024]{0:T(1024)S(1)}, f32[128]{0:T(128)S(1)}, f32[128,1024]{1,0:T(8,128)}) fusion(bf16[128,1024]{1,0:T(8,128)(2,1)S(1)} %copy-done.1, f32[128]{0:T(128)S(1)} %copy-done.50, f32[1024]{0:T(1024)S(1)} %bitcast.177, bf16[128,4224]{1,0:T(8,128)(2,1)S(1)} %concatenate.46, bf16[1024,4352]{1,0:T(8,128)(2,1)} %bitcast.157), kind=kOutput, calls=%fused_computation.98 | convolution fusion | flops 1108212608 | bytes 10527744 | tf_op jit(solution)/shard_map/dot_general | solution.py:109
  264.7 6.8 %convolution_convert_fusion.1 = bf16[1024,4096]{1,0:T(8,128)(2,1)} fusion(bf16[128,2048]{1,0:T(8,128)(2,1)} %copy-done.15, bf16[128,2048]{1,0:T(8,128)(2,1)S(1)} %copy-done.14, f32[128,1024]{1,0:T(8,128)S(1)} %get-tuple-element.99, f32[1024]{0:T(1024)S(1)} %bitcast.175, f32[128]{0:T(128)S(1)} %copy-done.46), kind=kOutput, calls=%fused_computation.4 | convolution fusion | flops 1080426496 | bytes 9966080 | tf_op jit(solution)/shard_map/dot_general | solution.py:103
  271.5 3.3 convolution_convert_fusion.3
  274.8 5.8 %convolution_convert_fusion = bf16[1024,4224]{1,0:T(8,128)(2,1)} fusion(bf16[128,4224]{1,0:T(8,128)(2,1)S(1)} %concatenate.46, bf16[128,1024]{1,0:T(8,128)(2,1)S(1)} %copy-done.1, f32[1024]{0:T(1024)S(1)} %bitcast.178, f32[128]{0:T(128)S(1)} %copy-done.50), kind=kOutput, calls=%fused_computation.1 | convolution fusion | flops 1112145920 | bytes 9998848 | tf_op jit(solution)/shard_map/dot_general | solution.py:103
  280.6 3.3 convolution_convert_fusion.2
  283.9 148.9 %reduce_grads.1 = (f32[32,4224]{1,0:T(8,128)S(1)}, f32[32,2048]{1,0:T(8,128)S(1)}, f32[32,4096]{1,0:T(8,128)S(1)}, f32[32,2048]{1,0:T(8,128)S(1)}, f32[88,128]{1,0:T(8,128)S(1)}) custom-call(bf16[4,2,2,2,32,4224]{5,4,3,2,1,0:T(8,128)(2,1)} %bitcast.151, bf16[4,2,2,2,32,2048]{5,4,3,2,1,0:T(8,128)(2,1)} %bitcast.153, ...), custom_call_target="tpu_custom_call" | custom-call | tf_op jit(solution)/shard_map/reduce_grads/pallas_call | solution.py:490
  441.4 4.4 fusion.8
  (234 shorter events, 67.0 us)
Async XLA Ops:
  0.7 152.7 %copy-start.1 = (bf16[128,1024]{1,0:T(8,128)(2,1)S(1)}, bf16[128,1024]{1,0:T(8,128)(2,1)}, u32[]{:S(2)}) copy-start(bf16[128,1024]{1,0:T(8,128)(2,1)} %param.19) | copy-start | bytes 786436
  165.4 14.0 %copy-start.22 = (bf16[128,1792]{1,0:T(8,128)(2,1)}, bf16[128,1792]{1,0:T(8,128)(2,1)S(1)}, u32[]{:S(2)}) copy-start(bf16[128,1792]{1,0:T(8,128)(2,1)S(1)} %get-tuple-element.57) | copy-start | bytes 1376260
  169.7 12.0 %copy-start.58 = (f32[24]{0:T(128)}, f32[24]{0:T(128)S(1)}, u32[]{:S(2)}) copy-start(f32[24]{0:T(128)S(1)} %exponential_negate_fusion) | copy-start | bytes 292
  171.0 10.7 %copy-start.23 = (f32[128,24]{1,0:T(8,128)}, f32[128,24]{1,0:T(8,128)S(1)}, u32[]{:S(2)}) copy-start(f32[128,24]{1,0:T(8,128)S(1)} %get-tuple-element.61) | copy-start | bytes 36868
  194.9 7.4 %copy-start.13 = (bf16[128,2048]{1,0:T(8,128)(2,1)}, bf16[128,2048]{1,0:T(8,128)(2,1)S(1)}, u32[]{:S(2)}) copy-start(bf16[128,2048]{1,0:T(8,128)(2,1)S(1)} %get-tuple-element.65) | copy-start | bytes 1572868
  194.9 7.4 %copy-start.15 = (bf16[128,2048]{1,0:T(8,128)(2,1)}, bf16[128,2048]{1,0:T(8,128)(2,1)S(1)}, u32[]{:S(2)}) copy-start(bf16[128,2048]{1,0:T(8,128)(2,1)S(1)} %get-tuple-element.66) | copy-start | bytes 1572868
  194.9 7.4 %copy-start.64 = (f32[128]{0:T(128)S(1)}, f32[128]{0:T(128)}, u32[]{:S(2)}) copy-start(f32[128]{0:T(128)} %copy-done.63) | copy-start | bytes 1540
  194.9 7.8 %copy-start = (bf16[4,2,2,2,32,2048]{5,4,3,2,1,0:T(8,128)(2,1)S(1)}, bf16[4,2,2,2,32,2048]{5,4,3,2,1,0:T(8,128)(2,1)}, u32[]{:S(2)}) copy-start(bf16[4,2,2,2,32,2048]{5,4,3,2,1,0:T(8,128)(2,1)} %get-tuple-element.28) | copy-start | bytes 12582916
  208.5 6.5 %copy-start.48 = (pred[128,128]{1,0:T(8,128)(4,1)S(1)}, pred[128,128]{1,0:T(8,128)(4,1)}, u32[]{:S(2)}) copy-start(pred[128,128]{1,0:T(8,128)(4,1)} %copy.133) | copy-start | bytes 49156
  208.5 6.5 %copy-start.51 = (f32[128,24]{0,1:T(8,128)S(1)}, f32[128,24]{0,1:T(8,128)}, u32[]{:S(2)}) copy-start(f32[128,24]{0,1:T(8,128)} %copy.131) | copy-start | bytes 36868
  208.5 6.5 %copy-start.52 = (f32[24,128]{1,0:T(8,128)S(1)}, f32[24,128]{1,0:T(8,128)}, u32[]{:S(2)}) copy-start(f32[24,128]{1,0:T(8,128)} %copy.134) | copy-start | bytes 36868
  208.5 6.5 %copy-start.66 = (f32[24]{0:T(128)S(1)}, f32[24]{0:T(128)}, u32[]{:S(2)}) copy-start(f32[24]{0:T(128)} %param.37) | copy-start | bytes 292
  257.0 7.3 %copy-start.62 = (f32[24]{0:T(128)S(1)}, f32[24]{0:T(128)}, u32[]{:S(2)}) copy-start(f32[24]{0:T(128)} %get-tuple-element.81) | copy-start | bytes 292
  257.1 7.3 %copy-start.68 = (f32[24]{0:T(128)S(1)}, f32[24]{0:T(128)}, u32[]{:S(2)}) copy-start(f32[24]{0:T(128)} %param.36) | copy-start | bytes 292
  257.1 7.3 %copy-start.42 = (f32[1536]{0:T(1024)S(1)}, f32[1536]{0:T(1024)}, u32[]{:S(2)}) copy-start(f32[1536]{0:T(1024)} %get-tuple-element.52) | copy-start | bytes 18436
  257.1 7.5 %copy-start.33 = (f32[7168]{0:T(1024)S(1)}, f32[7168]{0:T(1024)}, u32[]{:S(2)}) copy-start(f32[7168]{0:T(1024)} %reshape.390) | copy-start | bytes 86020
  257.1 7.5 %copy-start.41 = (f32[1792]{0:T(1024)S(1)}, f32[1792]{0:T(1024)}, u32[]{:S(2)}) copy-start(f32[1792]{0:T(1024)} %get-tuple-element.44) | copy-start | bytes 21508
  257.1 7.5 %copy-start.47 = (f32[1024]{0:T(1024)S(1)}, f32[1024]{0:T(1024)}, u32[]{:S(2)}) copy-start(f32[1024]{0:T(1024)} %get-tuple-element.42) | copy-start | bytes 12292
  257.1 7.5 %copy-start.59 = (f32[24]{0:T(128)S(1)}, f32[24]{0:T(128)}, u32[]{:S(2)}) copy-start(f32[24]{0:T(128)} %get-tuple-element.54) | copy-start | bytes 292
  257.1 7.6 %copy-start.14 = (bf16[128,2048]{1,0:T(8,128)(2,1)S(1)}, bf16[128,2048]{1,0:T(8,128)(2,1)}, u32[]{:S(2)}) copy-start(bf16[128,2048]{1,0:T(8,128)(2,1)} %copy-done.13) | copy-start | bytes 1572868
  257.1 7.5 %copy-start.46 = (f32[128]{0:T(128)S(1)}, f32[128]{0:T(128)}, u32[]{:S(2)}) copy-start(f32[128]{0:T(128)} %fusion.78) | copy-start | bytes 1540
  264.7 6.8 %copy-start.11 = (bf16[128,1536]{1,0:T(8,128)(2,1)S(1)}, bf16[128,1536]{1,0:T(8,128)(2,1)}, u32[]{:S(2)}) copy-start(bf16[128,1536]{1,0:T(8,128)(2,1)} %copy-done.10) | copy-start | bytes 1179652
  264.7 6.8 %copy-start.17 = (bf16[128,512]{1,0:T(8,128)(2,1)S(1)}, bf16[128,512]{1,0:T(8,128)(2,1)}, u32[]{:S(2)}) copy-start(bf16[128,512]{1,0:T(8,128)(2,1)} %copy.137) | copy-start | bytes 393220
  432.8 6.6 %copy-start.61 = (f32[128]{0:T(128)S(1)}, f32[128]{0:T(128)}, u32[]{:S(2)}) copy-start(f32[128]{0:T(128)} %copy-done.60) | copy-start | bytes 1540
  (45 other events, 141.2 us)
